TPU v7x, 512 devices: a whole 4x4x16 slice. The times are simulated.
512 devices in a mesh: tensor: 4 (over x), context: 8 (over y, core), dp: 16 (over z).
Axes of the slice: x: 4, y: 4, z: 16, core: 2. Of those that a mesh axis runs over, the one named last changes fastest.
Arguments:
- tokens: bfloat16 [32768, 3584], P(('tensor', 'context'), 'dp'), may hold values from -6 to 6
- route_ids: int32 [32768, 1], P(('tensor', 'context')), may hold values from 0 to 31; in each aligned block of 1024 rows (0 to 1023, 1024 to 2047, ...) at most 48 rows name the same one
- route_weights: float32 [32768, 1], P(('tensor', 'context')), may hold values from 0.2 to 1
- cotangent: bfloat16 [32768, 3584], P(('tensor', 'context'), 'dp'), may hold values from -6 to 6
- w_gate: bfloat16 [32, 2560, 3584], P(('tensor', 'context'), 'dp'), may hold values from -0.09375 to 0.09375
- w_up: bfloat16 [32, 2560, 3584], P(('tensor', 'context'), 'dp'), may hold values from -0.09375 to 0.09375
- w_down: bfloat16 [32, 3584, 2560], P(('tensor', 'context'), 'dp'), may hold values from -0.125 to 0.125
Outputs:
- mixed: bfloat16 [32768, 3584], P(('tensor', 'context'), 'dp')
- route_grad: float32 [32768, 1], P(('tensor', 'context'))
Inputs may be any that keep to these rules, and one draw needn't show every extreme that they name: `route_ids`: each row names one expert. In each aligned block of 1024 rows (the rows of one index of tensor+context) no expert is named by more than 48 routes, and in every draw some expert is named by exactly 48 routes of some block.
All inputs are finite; a program needn't handle non-finite values.
Results may differ from a plain program's by a relative error of at most 0.0057.
Values may be sent and summed in bfloat16 or wider, within the bound.
A program may use at most 64 MiB of HBM per device.

v0:
```python
import jax
import jax.numpy as jnp
from jax import lax
from jax.sharding import PartitionSpec as P


def dispatch_slots(slots):
    width = slots.shape[-1]
    moved = lax.all_to_all(slots, ("tensor", "context"), split_axis=0, concat_axis=0, tiled=True)
    return moved.reshape(-1, width)


def return_slots(slots):
    width = slots.shape[-1]
    moved = lax.all_to_all(slots, ("tensor", "context"), split_axis=0, concat_axis=0, tiled=True)
    return moved.reshape(-1, width)


def per_device(tokens, route_ids, route_weights, cotangent, w_gate, w_up, w_down):
    tensor_count = lax.axis_size("tensor")
    context_count = lax.axis_size("context")
    experts = tensor_count * context_count
    tok_rows, routes = route_ids.shape
    capacity = 3 * tok_rows * routes // (2 * experts)
    pair_count = tok_rows * routes
    features = tokens.shape[1]
    contract = (((1,), (1,)), ((), ()))
    flat_ids = route_ids.reshape(pair_count)
    onehot = (flat_ids[:, None] == jnp.arange(experts, dtype=jnp.int32)[None, :]).astype(jnp.int32)
    before = jnp.cumsum(onehot, axis=0) - onehot
    slot = flat_ids * capacity + jnp.sum(onehot * before, axis=1)
    placing = (jnp.arange(experts * capacity, dtype=jnp.int32)[:, None] == slot[None, :]).astype(
        jnp.bfloat16
    )
    token_pairs = jnp.repeat(tokens, routes, axis=0)
    cot_pairs = jnp.repeat(cotangent, routes, axis=0).astype(jnp.float32)
    placed_tokens = jnp.dot(placing, token_pairs, preferred_element_type=jnp.float32).astype(
        jnp.bfloat16
    )
    token_slots = dispatch_slots(placed_tokens.reshape(experts, capacity, features))
    gate_rows_local = w_gate[0]
    up_rows_local = w_up[0]
    down_local = w_down[0]
    model_width = gate_rows_local.shape[1]
    piece = lax.all_gather(token_slots, "dp", axis=1, tiled=True)
    gate = lax.dot_general(piece, gate_rows_local, contract, preferred_element_type=jnp.float32)
    up = lax.dot_general(piece, up_rows_local, contract, preferred_element_type=jnp.float32)
    hidden = (gate * jax.nn.sigmoid(gate) * up).astype(jnp.bfloat16)
    expert_out = lax.dot_general(
        lax.all_gather(hidden, "dp", axis=1, tiled=True),
        down_local,
        contract,
        preferred_element_type=jnp.float32,
    ).astype(jnp.bfloat16)
    out_back = return_slots(expert_out.reshape(experts, capacity, features))
    out_pairs = lax.dot_general(
        placing, out_back, (((0,), (0,)), ((), ())), preferred_element_type=jnp.float32
    )
    mixed = jnp.sum((route_weights * out_pairs).reshape(tok_rows, routes, features), axis=1).astype(
        jnp.bfloat16
    )
    partial_route = jnp.sum(out_pairs * cot_pairs, axis=1).reshape(tok_rows, routes)
    route_grad = lax.psum(partial_route, "dp") * model_width ** (-0.5)
    return (mixed, route_grad)


def solution(mesh):
    in_specs = (
        P(("tensor", "context"), "dp"),
        P(("tensor", "context"), None),
        P(("tensor", "context"), None),
        P(("tensor", "context"), "dp"),
        P(("tensor", "context"), "dp", None),
        P(("tensor", "context"), "dp", None),
        P(("tensor", "context"), "dp", None),
    )
    out_specs = (P(("tensor", "context"), "dp"), P(("tensor", "context"), None))
    return jax.shard_map(
        per_device, mesh=mesh, in_specs=in_specs, out_specs=out_specs, check_vma=False
    )
```

profile of v0, /device:TPU:1, one launch (start us, length us, event | category | flops | bytes accessed | tf_op | source)
XLA Modules:
  0.0 346.2 jit_solution(264137904184890030)
XLA Ops:
  7.2 0.0 copy-start
  7.2 0.0 all-gather.3.cloned.1.call-start
  7.2 0.8 fusion.13
  8.0 9.0 %reduce-window.6 = s32[32,8,128]{2,1,0:T(8,128)S(1)} reduce-window(s32[32,8,128]{2,1,0:T(8,128)S(1)} %fusion.13, s32[]{:T(128)} %constant.3.clone.1), window={size=1x1x128 pad=0_0x0_0x127_0}, to_apply=%region_0.0 | reduce-window | flops 4161536 | bytes 262148 | tf_op jit(solution)/shard_map/reduce-window
  17.0 0.1 slice.8
  17.1 0.1 copy.13
  17.3 0.1 copy.14
  17.4 0.1 broadcast_add_fusion
  17.5 0.7 fusion.12
  18.2 0.7 multiply_add_fusion
  18.9 2.5 fusion.4
  21.4 0.3 copy.15
  21.7 23.9 %all_to_all.10 = bf16[32,48,224]{2,1,0:T(8,128)(2,1)S(1)} all-to-all(bf16[32,48,224]{2,1,0:T(8,128)(2,1)S(1)} %bitcast.40), channel_id=1, replica_groups=mesh['tensor'=4,'context'=8,'dp'=16] {'tensor','context'}, dimensions={0} | all-to-all | bytes 1376256 | tf_op jit(solution)/shard_map/all_to_all | solution.py:9
  45.6 1.1 copy.16
  46.7 0.0 all-gather.3.cloned.1.call-update
  46.7 0.0 copy-start.2
  46.7 0.0 all-gather.5.cloned.1.call-start
  46.8 131.7 %all-gather.3.cloned.1.call-done = bf16[1536,3584]{0,1:T(8,128)(2,1)} async-done(((bf16[1536,224]{0,1:T(8,128)(2,1)}), bf16[1536,3584]{0,1:T(8,128)(2,1)}) %all-gather.3.cloned.1.call-update) | async-done | bytes 11010064 | tf_op jit(solution)/shard_map/all_gather | solution.py:45
  178.5 0.0 copy-start.1
  178.5 6.6 %fusion.8 = f32[1536,160]{0,1:T(8,128)S(1)} fusion(bf16[1536,3584]{0,1:T(8,128)(2,1)} %all-gather.3.cloned.1.call-done, bf16[1,160,3584]{2,1,0:T(8,128)(2,1)} %param.11), kind=kOutput, calls=%fused_computation.11 | convolution fusion | flops 1761607680 | bytes 13139968 | tf_op jit(solution)/shard_map/dot_general | solution.py:46
  185.0 0.0 copy-done.2
  185.0 1.0 copy-done.1
  186.1 2.8 fusion.5
  188.8 0.0 all-gather.5.cloned.1.call-update
  188.9 98.8 %all-gather.5.cloned.1.call-done = bf16[1536,2560]{0,1:T(8,128)(2,1)} async-done(((bf16[1536,160]{0,1:T(8,128)(2,1)}), bf16[1536,2560]{0,1:T(8,128)(2,1)}) %all-gather.5.cloned.1.call-update) | async-done | bytes 7864336 | tf_op jit(solution)/shard_map/all_gather | solution.py:50
  287.6 0.0 copy-done
  287.6 5.2 %convolution_convert_fusion = bf16[1536,224]{0,1:T(8,128)(2,1)S(1)} fusion(bf16[1536,2560]{0,1:T(8,128)(2,1)} %all-gather.5.cloned.1.call-done, bf16[1,224,2560]{2,1,0:T(8,128)(2,1)S(1)} %copy-done), kind=kOutput, calls=%fused_computation.7 | convolution fusion | flops 1761951744 | bytes 9699328 | tf_op jit(solution)/shard_map/dot_general | solution.py:49
  292.8 0.0 copy-start.3
  292.8 0.0 copy-start.4
  292.8 0.3 copy.17
  293.1 21.6 %all_to_all.11 = bf16[32,48,224]{2,1,0:T(8,128)(2,1)S(1)} all-to-all(bf16[32,48,224]{2,1,0:T(8,128)(2,1)S(1)} %bitcast.42), channel_id=1, replica_groups=mesh['tensor'=4,'context'=8,'dp'=16] {'tensor','context'}, dimensions={0} | all-to-all | bytes 1376256 | tf_op jit(solution)/shard_map/all_to_all | solution.py:15
  314.6 0.0 copy-done.3
  314.7 0.0 copy-done.4
  314.7 2.1 multiply_reduce_fusion
  316.8 21.9 %psum.7 = f32[1024,1]{0,1:T(1,128)S(1)} all-reduce(f32[1024,1]{0,1:T(1,128)S(1)} %bitcast.49), channel_id=1, replica_groups=mesh['tensor'=4,'context'=8,'dp'=16] {'dp'}, use_global_device_ids=true, to_apply=%region_4.5 | all-reduce | flops 1024 | bytes 8192 | tf_op jit(solution)/shard_map/psum | solution.py:63
  338.7 0.6 broadcast_multiply_fusion
  (2 shorter events, 0.0 us)
Async XLA Ops:
  7.2 280.5 %copy-start = (bf16[1,224,2560]{2,1,0:T(8,128)(2,1)S(1)}, bf16[1,224,2560]{2,1,0:T(8,128)(2,1)}, u32[]{:S(2)}) copy-start(bf16[1,224,2560]{2,1,0:T(8,128)(2,1)} %param.13) | copy-start | bytes 3440644
  7.2 171.3 %all-gather.3.cloned.1.call-start = ((), (), s32[]{:S(2)}) async-start(), calls=%async_computation.2 | async-start | bytes 11698176 | tf_op jit(solution)/shard_map/all_gather | solution.py:45
  46.7 138.3 %copy-start.2 = (bf16[1,160,3584]{2,1,0:T(8,128)(2,1)S(1)}, bf16[1,160,3584]{2,1,0:T(8,128)(2,1)}, u32[]{:S(2)}) copy-start(bf16[1,160,3584]{2,1,0:T(8,128)(2,1)} %param.12) | copy-start | bytes 3440644
  46.7 240.9 %all-gather.5.cloned.1.call-start = ((), (), s32[]{:S(2)}) async-start(), calls=%async_computation.3 | async-start | bytes 8355840 | tf_op jit(solution)/shard_map/all_gather | solution.py:50
  178.5 7.6 %copy-start.1 = (bf16[1536,3584]{0,1:T(8,128)(2,1)S(1)}, bf16[1536,3584]{0,1:T(8,128)(2,1)}, u32[]{:S(2)}) copy-start(bf16[1536,3584]{0,1:T(8,128)(2,1)} %all-gather.3.cloned.1.call-done) | copy-start | bytes 33030148
  292.8 21.9 %copy-start.3 = (bf16[1024,224]{0,1:T(8,128)(2,1)S(1)}, bf16[1024,224]{0,1:T(8,128)(2,1)}, u32[]{:S(2)}) copy-start(bf16[1024,224]{0,1:T(8,128)(2,1)} %param.10) | copy-start | bytes 1376260
  292.8 21.9 %copy-start.4 = (f32[1024,1]{0,1:T(1,128)S(1)}, f32[1024,1]{0,1:T(1,128)}, u32[]{:S(2)}) copy-start(f32[1024,1]{0,1:T(1,128)} %param.9) | copy-start | bytes 12292
Sparse Core Ops, SparseCore 0:
  46.9 131.5 all-gather.2
  189.0 98.5 all-gather.4
where the time goes:
time: 351 us; the launch traced here: 346 us
  waiting for transfers between devices  230 us (66%)
  blocking collectives  67.4 us (19%)
  matrix products  19.1 us (5%)
  between operations  14.1 us (4%)
  other arithmetic  12 us (3%)
    all_gather x1, waiting for transfers between devices, per_device(): piece = lax.all_gather(token_slots, 'dp', axis=1, tiled=True)  132 us
    all_gather x1, waiting for transfers between devices, per_device(): lax.all_gather(hidden, 'dp', axis=1, tiled=True)  98.8 us
    all_to_all x1, blocking collectives, dispatch_slots(): lax.all_to_all(slots, ('tensor', 'context'), split_axis=0, concat_axis=0,...  23.9 us
    psum x1, blocking collectives, per_device(): route_grad = lax.psum(partial_route, 'dp') * model_width ** (-0.5)  21.9 us
    all_to_all x1, blocking collectives, return_slots(): lax.all_to_all(slots, ('tensor', 'context'), split_axis=0, concat_axis=0,...  21.6 us
    another operation x3, other arithmetic  9.15 us
  transfers between devices with their start and end apart: 2, of which 2 were waited for; matrix products, arithmetic and copies ran while one was open for 0% of the time, Pallas kernels for 0%

commit v1 on v0

v1 whole, which is shorter than its diff:
```python
import jax
import jax.numpy as jnp
from jax import lax
from jax.experimental import pallas as pl
from jax.experimental.pallas import tpu as pltpu
from jax.sharding import PartitionSpec as P

MESH = pl.DeviceIdType.MESH
F32, BF16 = jnp.float32, jnp.bfloat16
NX, NC, NZ = 4, 8, 16
ROWS, FEAT, HID, D = 1024, 224, 160, 3584
CAP = 48
XSLOTS = NC * CAP
GX = 2
GROUP = GX * XSLOTS
GROUPS = NX // GX
TILE = 128
NT = (((1,), (1,)), ((), ()))
TOK_PIECES = ((0, 64), (64, 48), (112, 64), (176, 48))
HID_PIECES = ((0, 48), (48, 32), (80, 48), (128, 32))
PIECES = len(TOK_PIECES)
UP_LAST = range(PIECES // 2)
DOWN_LAST = range(PIECES // 2, PIECES)


def kernel(
    ids_ref, wts_ref, tok_in, cot_ref, wg_hbm, wu_hbm, wd_hbm,
    mix_ref, route_ref,
    wg, wu, wd, place, xs, xr, tok, hid, outs, ret, pairs, parts,
    w_sem, x_send, x_recv, t_send, t_recv, h_send, h_recv, o_send, o_recv, p_send, p_recv,
):
    mx, mc, mz = lax.axis_index("tensor"), lax.axis_index("context"), lax.axis_index("dp")
    above, below = lax.rem(mz + 1, NZ), lax.rem(mz + NZ - 1, NZ)

    barrier = pltpu.get_barrier_semaphore()

    def greet(k, carry):
        p = lax.rem(mx * NC + mc + k, NX * NC)
        pl.semaphore_signal(barrier, inc=1, device_id=(p // NC, lax.rem(p, NC), mz), device_id_type=MESH)
        return carry

    def greet_z(k, carry):
        pl.semaphore_signal(barrier, inc=1, device_id=(mx, mc, lax.rem(mz + k, NZ)), device_id_type=MESH)
        return carry

    lax.fori_loop(1, NX * NC, greet, 0)
    lax.fori_loop(1, NZ, greet_z, 0)
    loads = [
        pltpu.make_async_copy(src, dst, w_sem.at[i])
        for i, (src, dst) in enumerate(((wg_hbm, wg), (wu_hbm, wu), (wd_hbm, wd)))
    ]
    for load in loads:
        load.start()

    ids = ids_ref[...]
    rel = lax.rem(mx + NX - ids // NC, NX) * NC + lax.rem(ids, NC)
    expert = lax.broadcasted_iota(jnp.int32, (NX * NC, TILE), 0)
    lower = (
        lax.broadcasted_iota(jnp.int32, (TILE, TILE), 0) < lax.broadcasted_iota(jnp.int32, (TILE, TILE), 1)
    ).astype(F32).astype(BF16)
    seen = jnp.zeros((NX * NC, 1), F32)
    slots = []
    for i in range(ROWS // TILE):
        r = rel[:, i * TILE : (i + 1) * TILE]
        onehot = (expert == r).astype(F32)
        before = jnp.dot(onehot.astype(BF16), lower, preferred_element_type=F32) + seen
        position = jnp.sum(onehot * before, axis=0, keepdims=True)
        slots.append(r * CAP + position.astype(jnp.int32))
        seen = seen + jnp.sum(onehot, axis=1, keepdims=True)
    slot = jnp.concatenate(slots, axis=1)

    def place_rows(j):
        at = lax.broadcasted_iota(jnp.int32, (XSLOTS, ROWS), 0) + j * XSLOTS
        rows = pl.ds(j * XSLOTS, XSLOTS)
        place[rows, :] = (at == slot).astype(F32).astype(BF16)
        xs[rows, :] = lax.dot_general(place[rows, :], tok_in[...], NT, preferred_element_type=F32).astype(BF16)

    def piece_at(j, c):
        return pl.ds(pl.multiple_of((j * NC + c) * CAP, 16), CAP)

    def scatter(src, dst, send, recv, j, toward):
        tx = lax.rem(mx + NX + toward * j, NX)

        def one(k, carry):
            c = lax.rem(mc + k, NC)
            pltpu.make_async_remote_copy(
                src_ref=src.at[piece_at(j, c), :],
                dst_ref=dst.at[piece_at(j, mc), :],
                send_sem=send,
                recv_sem=recv.at[j // GX],
                device_id=(tx, c, mz),
                device_id_type=MESH,
            ).start()
            return carry

        if j == 0:
            pltpu.make_async_copy(src.at[piece_at(0, mc), :], dst.at[piece_at(0, mc), :], recv.at[0]).start()
        lax.fori_loop(1 if j == 0 else 0, NC, one, 0)

    def scattered(dst, recv, g):
        part = dst.at[pl.ds(g * GROUP, GROUP), :]
        pltpu.make_async_copy(part, part, recv.at[g]).wait()

    def all_sent(buf, send):
        part = buf.at[pl.ds(CAP, (NX * NC - 1) * CAP), :]
        pltpu.make_async_copy(part, part, send).wait()

    def ring(buf, send, recv, pieces, g, way, s, p):
        origin = lax.rem(mz + NZ - s, NZ) if way == 0 else lax.rem(mz + s, NZ)
        start, size = pieces[p]
        part = buf.at[g, origin, pl.ds(start, size), :]
        return pltpu.make_async_remote_copy(
            src_ref=part,
            dst_ref=part,
            send_sem=send.at[g],
            recv_sem=recv.at[g, way, s, p],
            device_id=(mx, mc, above if way == 0 else below),
            device_id_type=MESH,
        )

    def arrived(buf, send, recv, pieces, g, way, s, p):
        origin = lax.rem(mz + NZ - s, NZ) if way == 0 else lax.rem(mz + s, NZ)
        start, size = pieces[p]
        part = buf.at[g, origin, pl.ds(start, size), :]
        pltpu.make_async_copy(part, part, recv.at[g, way, s - 1, p]).wait()

    def begin(phase):
        for p in range(PIECES):
            for way in range(2):
                ring(*phase, way, 0, p).start()

    def run(phase, work, after):
        def step(s, carry):
            for p in range(PIECES):
                for way in range(2):
                    arrived(*phase, way, s, p)
                    ring(*phase, way, s, p).start()
            work(s - 1)
            return carry

        lax.fori_loop(1, NZ // 2 - 1, step, 0)
        s = NZ // 2 - 1
        for p in range(PIECES):
            for way in range(2):
                arrived(*phase, way, s, p)
                if p in (UP_LAST if way == 0 else DOWN_LAST):
                    ring(*phase, way, s, p).start()
        after()
        for p in range(PIECES // 2):
            arrived(*phase, 0, NZ // 2, UP_LAST[p])
            arrived(*phase, 1, NZ // 2, DOWN_LAST[p])

    def ring_sent(phase):
        buf, send, _, _, g = phase
        part = buf.at[g, pl.ds(0, NZ - 1)]
        pltpu.make_async_copy(part, part, send.at[g]).wait()

    tok_phase = [(tok, t_send, t_recv, TOK_PIECES, g) for g in range(GROUPS)]
    hid_phase = [(hid, h_send, h_recv, HID_PIECES, g) for g in range(GROUPS)]

    def turn_in(g):
        tok[g, mz] = xr[pl.ds(g * GROUP, GROUP), :].astype(F32).T.astype(BF16)

    def expert_in(g, i):
        cols = pl.ds(pl.multiple_of(i * TILE, TILE), TILE)
        x = tok[g, :, :, cols].reshape(NZ * FEAT, TILE)
        gate = jnp.dot(wg[...], x, preferred_element_type=F32)
        up = jnp.dot(wu[...], x, preferred_element_type=F32)
        hid[g, mz, :, cols] = (gate * jax.nn.sigmoid(gate) * up).astype(BF16)

    def expert_out(g, i):
        cols = pl.ds(pl.multiple_of(i * TILE, TILE), TILE)
        h = hid[g, :, :, cols].reshape(NZ * HID, TILE)
        out = jnp.dot(wd[...], h, preferred_element_type=F32).astype(BF16).astype(F32)
        outs[pl.ds(pl.multiple_of(g * GROUP + i * TILE, TILE), TILE), :] = out.T.astype(BF16)

    def unplace(g):
        rows = pl.ds(g * GROUP, GROUP)
        got = ret[rows, :].astype(F32).T.astype(BF16)
        return jnp.dot(got, place[rows, :], preferred_element_type=F32)

    pl.semaphore_wait(barrier, NX * NC - 1 + NZ - 1)
    for j in range(NX):
        place_rows(j)
        scatter(xs, xr, x_send, x_recv, j, -1)
    scattered(xr, x_recv, 0)
    turn_in(0)
    begin(tok_phase[0])
    scattered(xr, x_recv, 1)
    turn_in(1)
    for load in loads:
        load.wait()

    run(tok_phase[0], lambda i: None, lambda: begin(tok_phase[1]))
    run(tok_phase[1], lambda i: expert_in(0, i), lambda: begin(hid_phase[0]))
    run(hid_phase[0], lambda i: expert_in(1, i), lambda: begin(hid_phase[1]))

    def send_back(g):
        for j in range(g * GX, (g + 1) * GX):
            scatter(outs, ret, o_send, o_recv, j, 1)

    run(hid_phase[1], lambda i: expert_out(0, i), lambda: send_back(0))

    def tail(i, carry):
        expert_out(1, i)
        return carry

    lax.fori_loop(0, GROUP // TILE, tail, 0)
    send_back(1)
    scattered(ret, o_recv, 0)
    pairs[...] = unplace(0)
    scattered(ret, o_recv, 1)
    pairs[...] += unplace(1)
    for i in range(ROWS // TILE):
        cols = pl.ds(i * TILE, TILE)
        parts[mz, pl.ds(i, 1), :] = jnp.sum(pairs[:, cols] * cot_ref[:, cols].astype(F32), axis=0, keepdims=True)

    def share(k, carry):
        pltpu.make_async_remote_copy(
            src_ref=parts.at[mz],
            dst_ref=parts.at[mz],
            send_sem=p_send,
            recv_sem=p_recv,
            device_id=(mx, mc, lax.rem(mz + k, NZ)),
            device_id_type=MESH,
        ).start()
        return carry

    lax.fori_loop(1, NZ, share, 0)
    mix_ref[...] = (pairs[...] * wts_ref[...]).astype(BF16)
    all_sent(xs, x_send)
    all_sent(outs, o_send)
    for phase in tok_phase + hid_phase:
        ring_sent(phase)
    others = parts.at[pl.ds(0, NZ - 1)]
    pltpu.make_async_copy(others, others, p_recv).wait()
    pltpu.make_async_copy(others, others, p_send).wait()
    route_ref[...] = jnp.sum(parts[...], axis=0) * D ** (-0.5)


def per_device(tokens, route_ids, route_weights, cotangent, w_gate, w_up, w_down):
    vmem, hbm = pl.BlockSpec(memory_space=pltpu.VMEM), pl.BlockSpec(memory_space=pl.ANY)
    dma, slots = pltpu.SemaphoreType.DMA, NX * NC * CAP
    mixed, route = pl.pallas_call(
        kernel,
        out_shape=(jax.ShapeDtypeStruct((FEAT, ROWS), BF16), jax.ShapeDtypeStruct((8, TILE), F32)),
        in_specs=[vmem] * 4 + [hbm] * 3,
        out_specs=(vmem, vmem),
        scratch_shapes=[
            pltpu.VMEM((HID, D), BF16),
            pltpu.VMEM((HID, D), BF16),
            pltpu.VMEM((FEAT, NZ * HID), BF16),
            pltpu.VMEM((slots, ROWS), BF16),
            pltpu.VMEM((slots, FEAT), BF16),
            pltpu.VMEM((slots, FEAT), BF16),
            pltpu.VMEM((GROUPS, NZ, FEAT, GROUP), BF16),
            pltpu.VMEM((GROUPS, NZ, HID, GROUP), BF16),
            pltpu.VMEM((slots, FEAT), BF16),
            pltpu.VMEM((slots, FEAT), BF16),
            pltpu.VMEM((FEAT, ROWS), F32),
            pltpu.VMEM((NZ, 8, TILE), F32),
            dma((3,)),
            dma,
            dma((GROUPS,)),
            dma((GROUPS,)),
            dma((GROUPS, 2, NZ // 2, PIECES)),
            dma((GROUPS,)),
            dma((GROUPS, 2, NZ // 2, PIECES)),
            dma,
            dma((GROUPS,)),
            dma,
            dma,
        ],
        compiler_params=pltpu.CompilerParams(
            collective_id=0, has_side_effects=True, vmem_limit_bytes=52 * 2**20
        ),
    )(
        route_ids.reshape(1, ROWS),
        route_weights.reshape(1, ROWS),
        tokens.T,
        cotangent.T,
        w_gate[0],
        w_up[0],
        w_down[0],
    )
    return mixed.T, route.reshape(ROWS, 1)


def solution(mesh):
    in_specs = (
        P(("tensor", "context"), "dp"),
        P(("tensor", "context"), None),
        P(("tensor", "context"), None),
        P(("tensor", "context"), "dp"),
        P(("tensor", "context"), "dp", None),
        P(("tensor", "context"), "dp", None),
        P(("tensor", "context"), "dp", None),
    )
    out_specs = (P(("tensor", "context"), "dp"), P(("tensor", "context"), None))
    return jax.shard_map(
        per_device, mesh=mesh, in_specs=in_specs, out_specs=out_specs, check_vma=False
    )
```

time: 351 us -> 249 us (0.71); the launches traced: 346 us -> 248 us
  Pallas kernels: 0 us -> 243 us
  waiting for transfers between devices: 230 us -> 0 us
  blocking collectives: 67.4 us -> 0 us
  matrix products: 19.1 us -> 0 us
  between operations: 14.1 us -> 0.65 us
  other arithmetic: 12 us -> 0 us
    pallas_call x0 -> x1, Pallas kernels: none -> 243 us  [per_device(): pl.pallas_call(kernel, out_shape=(jax.ShapeDtypeStruct((FEAT, ROWS), BF16...]
    all_gather x2 -> x0, waiting for transfers between devices: 230 us -> none  [the longest x1 132 us: per_device(): piece = lax.all_gather(token_slots, 'dp', axis=1, tiled=True)]
    all_to_all x2 -> x0, blocking collectives: 45.4 us -> none  [the longest x1 23.9 us: dispatch_slots(): lax.all_to_all(slots, ('tensor', 'context'), split_axis=0, concat_axis=0,...]
    psum x1 -> x0, blocking collectives: 21.9 us -> none  [per_device(): route_grad = lax.psum(partial_route, 'dp') * model_width ** (-0.5)]
    dot_general x5 -> x0, matrix products: 19.1 us -> none  [the longest x1 6.56 us: per_device(): lax.dot_general(piece, gate_rows_local, contract, preferred_element_type=...]
    another operation x3 -> x0, other arithmetic: 9.15 us -> none
    unnamed x10, local copies, waits for them, and re-layouts: 1.06 us -> 4.76 us
  transfers between devices with their start and end apart: 2 -> 0, of which waited for: 2 -> 0; matrix products, arithmetic and copies ran while one was open for 0% -> 0% of each run, Pallas kernels for 0% -> 0%
where the time goes in v1:
time: 249 us; the launch traced here: 248 us
  Pallas kernels  243 us (98%)
  local copies, waits for them, and re-layouts  4.76 us (2%)
    pallas_call x1, Pallas kernels, per_device(): pl.pallas_call(kernel, out_shape=(jax.ShapeDtypeStruct((FEAT, ROWS), BF16...  243 us

profile of v1, /device:TPU:1, one launch (start us, length us, event | category | flops | bytes accessed | tf_op | source)
XLA Modules:
  0.0 248.3 jit_solution(1170706010193986331)
XLA Ops:
  0.6 0.0 copy-start
  0.6 1.0 copy-done
  1.7 0.0 copy-start.1
  1.7 1.0 copy-done.1
  2.7 0.0 copy-start.2
  2.7 0.7 copy-done.2
  3.4 0.0 copy-start.3
  3.4 0.7 copy-done.3
  4.0 242.9 %shard_map.86 = (bf16[224,1024]{1,0:T(8,128)(2,1)S(1)}, f32[8,128]{1,0:T(8,128)S(1)}) custom-call(s32[1,1024]{1,0:T(1,128)S(1)} %bitcast.13, f32[1,1024]{1,0:T(1,128)S(1)} %bitcast.14, bf16[224,1024]{1,0:T(8,128)(2,1)S(1)} %bitcast.9, bf16[224,1024]{1,0:T(8,128)(2,1)S(1)} %bitcast.10, bf16[160,3584]{1,0:T(8,128)(2,1)} %bitcast.15, ...), custom_call_target="tpu_custom_call" | custom-call | tf_op jit(solution)/shard_map/pallas_call | solution.py:244
  247.0 0.8 copy.11
  247.7 0.6 copy.12
Async XLA Ops:
  0.6 1.0 copy-start
  1.7 1.0 copy-start.1
  2.7 0.7 copy-start.2
  3.4 0.7 copy-start.3

commit v2 on v1

v2 whole, which is shorter than its diff:
```python
import jax
import jax.numpy as jnp
from jax import lax
from jax.experimental import pallas as pl
from jax.experimental.pallas import tpu as pltpu
from jax.sharding import PartitionSpec as P

MESH = pl.DeviceIdType.MESH
F32, BF16 = jnp.float32, jnp.bfloat16
NX, NC, NZ = 4, 8, 16
ROWS, FEAT, HID, D = 1024, 224, 160, 3584
CAP = 48
XSLOTS = NC * CAP
GX = 2
GROUP = GX * XSLOTS
GROUPS = NX // GX
SLOTS = NX * XSLOTS
TILE = 128
NT = (((1,), (1,)), ((), ()))
PLAIN = 128
SLOTTED = FEAT - PLAIN
PAIR = 2 * PLAIN
STEPS = NZ // 2
FAR = (STEPS - 1) * PAIR
PLAIN_PIECES = tuple((32 * p, 32, 0, ROWS) for p in range(4))
SLOTTED_PIECES = tuple((48 * (p % 2), 48, GROUP * (p // 2), GROUP) for p in range(4))
HID_PIECES = tuple((80 * (p % 2), 80, XSLOTS * (p // 2), XSLOTS) for p in range(4))
PIECES = 4


def kernel(
    ids_ref, wts_ref, tok_in, cot_ref, wg_hbm, wu_hbm, wd_hbm,
    mix_ref, route_ref,
    wg, wu, wd, w_placed, w_slot, place, xs, xr, ps, pr, plain, slotted, acc, hid, outs, ret, pairs, parts,
    w_sem, x_send, x_recv, ps_send, ps_recv, a_send, a_recv, b_send, b_recv, h_send, h_recv,
    o_send, o_recv, p_send, p_recv,
):
    mx, mc, mz = lax.axis_index("tensor"), lax.axis_index("context"), lax.axis_index("dp")
    above, below = lax.rem(mz + 1, NZ), lax.rem(mz + NZ - 1, NZ)

    barrier = pltpu.get_barrier_semaphore()

    def greet(k, carry):
        p = lax.rem(mx * NC + mc + k, NX * NC)
        pl.semaphore_signal(barrier, inc=1, device_id=(p // NC, lax.rem(p, NC), mz), device_id_type=MESH)
        return carry

    def greet_z(k, carry):
        pl.semaphore_signal(barrier, inc=1, device_id=(mx, mc, lax.rem(mz + k, NZ)), device_id_type=MESH)
        return carry

    lax.fori_loop(1, NZ, greet_z, 0)
    lax.fori_loop(1, NX * NC, greet, 0)
    loads = [
        pltpu.make_async_copy(src, dst, w_sem.at[i])
        for i, (src, dst) in enumerate(((wg_hbm, wg), (wu_hbm, wu), (wd_hbm, wd)))
    ]
    for load in loads:
        load.start()

    ids = ids_ref[...]
    rel = lax.rem(mx + NX - ids // NC, NX) * NC + lax.rem(ids, NC)
    expert = lax.broadcasted_iota(jnp.int32, (NX * NC, TILE), 0)
    lower = (
        lax.broadcasted_iota(jnp.int32, (TILE, TILE), 0) < lax.broadcasted_iota(jnp.int32, (TILE, TILE), 1)
    ).astype(F32).astype(BF16)
    seen = jnp.zeros((NX * NC, 1), F32)
    slots = []
    for i in range(ROWS // TILE):
        r = rel[:, i * TILE : (i + 1) * TILE]
        onehot = (expert == r).astype(F32)
        before = jnp.dot(onehot.astype(BF16), lower, preferred_element_type=F32) + seen
        position = jnp.sum(onehot * before, axis=0, keepdims=True)
        slots.append(r * CAP + position.astype(jnp.int32))
        seen = seen + jnp.sum(onehot, axis=1, keepdims=True)
    slot = jnp.concatenate(slots, axis=1)

    def piece_at(j, c):
        return pl.ds(pl.multiple_of((j * NC + c) * CAP, 16), CAP)

    def scatter(src, dst, send, recv, j, toward, lanes):
        tx = lax.rem(mx + NX + toward * j, NX)

        def one(k, carry):
            c = lax.rem(mc + k, NC)
            pltpu.make_async_remote_copy(
                src_ref=src.at[piece_at(j, c), lanes],
                dst_ref=dst.at[piece_at(j, mc), lanes],
                send_sem=send,
                recv_sem=recv,
                device_id=(tx, c, mz),
                device_id_type=MESH,
            ).start()
            return carry

        if j == 0:
            pltpu.make_async_copy(src.at[piece_at(0, mc), lanes], dst.at[piece_at(0, mc), lanes], recv).start()
        lax.fori_loop(1 if j == 0 else 0, NC, one, 0)

    def wait_for(part, sem):
        pltpu.make_async_copy(part, part, sem).wait()

    def offset_rows(j):
        return pl.ds(j * XSLOTS, XSLOTS)

    def group_rows(g):
        return pl.ds(g * GROUP, GROUP)

    def part_of(ring, way, s, p):
        origin = lax.rem(mz + NZ - s, NZ) if way == 0 else lax.rem(mz + s, NZ)
        r, rows, c, cols = ring["pieces"][p]
        return ring["buf"].at[(*ring["at"], origin, pl.ds(r, rows), pl.ds(c, cols))]

    def forward(ring, way, s, p):
        part = part_of(ring, way, s, p)
        src = part
        if isinstance(s, int) and s == 0 and "own" in ring:
            r, rows, c, cols = ring["pieces"][p]
            src = ring["own"].at[pl.ds(r, rows), pl.ds(c, cols)]
        pltpu.make_async_remote_copy(
            src_ref=src,
            dst_ref=part,
            send_sem=ring["send"],
            recv_sem=ring["recv"].at[(*ring["at"], way, s, p)],
            device_id=(mx, mc, above if way == 0 else below),
            device_id_type=MESH,
        ).start()

    def arrived(ring, way, s, p):
        wait_for(part_of(ring, way, s, p), ring["recv"].at[(*ring["at"], way, s - 1, p)])

    def begin(ring):
        for p in range(PIECES):
            for way in range(2):
                forward(ring, way, 0, p)

    def run(ring, work, after):
        def step(s, carry):
            for p in range(PIECES):
                for way in range(2):
                    arrived(ring, way, s, p)
                    forward(ring, way, s, p)
            work(s)
            return carry

        lax.fori_loop(1, STEPS - 1, step, 0)
        for p in range(PIECES):
            for way in range(2):
                arrived(ring, way, STEPS - 1, p)
                if p % 2 == way:
                    forward(ring, way, STEPS - 1, p)
        after()

    def last(ring, p):
        arrived(ring, p % 2, STEPS, p)

    def ring_sent(ring):
        wait_for(ring["buf"].at[(*ring["at"], pl.ds(0, NZ - 1))], ring["send"])

    plain_ring = dict(buf=plain, at=(), send=a_send, recv=a_recv, pieces=PLAIN_PIECES, own=tok_in)
    slotted_ring = dict(buf=slotted, at=(), send=b_send, recv=b_recv, pieces=SLOTTED_PIECES)
    hid_rings = [
        dict(buf=hid, at=(g,), send=h_send.at[g], recv=h_recv, pieces=HID_PIECES) for g in range(GROUPS)
    ]

    def put_own(j):
        rows = offset_rows(j)
        at = lax.broadcasted_iota(jnp.int32, (XSLOTS, ROWS), 0) + j * XSLOTS
        place[rows, :] = (at == slot).astype(F32).astype(BF16)
        xs[rows, :] = lax.dot_general(place[rows, :], tok_in[...], NT, preferred_element_type=F32).astype(BF16)
        scatter(xs, xr, x_send, x_recv.at[j // GX], j, -1, pl.ds(0, FEAT))

    def put_pair(j, s):
        lanes = pl.ds(pl.multiple_of((s - 1) * PAIR, PAIR), PAIR)
        rows = offset_rows(j)
        pair = jnp.concatenate([plain[lax.rem(mz + NZ - s, NZ)], plain[lax.rem(mz + s, NZ)]], axis=0)
        ps[rows, lanes] = lax.dot_general(place[rows, :], pair, NT, preferred_element_type=F32).astype(BF16)
        scatter(ps, pr, ps_send, ps_recv.at[j // GX], j, -1, lanes)

    def put_far(j):
        lanes = pl.ds(FAR, PLAIN)
        rows = offset_rows(j)
        far = plain[lax.rem(mz + STEPS, NZ)]
        ps[rows, lanes] = lax.dot_general(place[rows, :], far, NT, preferred_element_type=F32).astype(BF16)
        scatter(ps, pr, ps_send, ps_recv.at[j // GX], j, -1, lanes)

    def sort_weights(planes):
        for o in planes:
            away = lax.rem(o + NZ - mz, NZ)
            half = away // STEPS
            lane = lax.rem((1 - half) * (PAIR * away - PLAIN) + half * PAIR * (NZ - 1 - away) + NZ * PLAIN, NZ * PLAIN)
            at = pl.ds(pl.multiple_of(lane, TILE), PLAIN)
            for rows, w in ((pl.ds(0, HID), wg), (pl.ds(HID, HID), wu)):
                w_placed[rows, at] = w[:, o * FEAT : o * FEAT + PLAIN]
                w_slot[rows, o * SLOTTED : (o + 1) * SLOTTED] = w[:, o * FEAT + PLAIN : (o + 1) * FEAT]

    def turn_in(g):
        slotted[mz, :, g * GROUP : (g + 1) * GROUP] = xr[group_rows(g), pl.ds(PLAIN, SLOTTED)].astype(F32).T.astype(BF16)

    def placed_in(g, i):
        start = pl.multiple_of(g * GROUP + i * TILE, TILE)
        rows, cols = pl.ds(start, TILE), pl.ds(start, TILE)
        acc[:, cols] = lax.dot_general(
            w_placed[:, pl.ds(0, FAR + PLAIN)], pr[rows, :], NT, preferred_element_type=F32
        ) + lax.dot_general(
            w_placed[:, pl.ds(FAR + PLAIN, PLAIN)], xr[rows, pl.ds(0, PLAIN)], NT, preferred_element_type=F32
        )

    def slotted_in(g, i):
        start = pl.multiple_of(g * GROUP + i * TILE, TILE)
        cols = pl.ds(start, TILE)
        x = slotted[:, :, cols].reshape(NZ * SLOTTED, TILE)
        both = acc[:, cols] + jnp.dot(w_slot[...], x, preferred_element_type=F32)
        gate, up = both[:HID], both[HID:]
        hid[g, mz, :, pl.ds(pl.multiple_of(i * TILE, TILE), TILE)] = (gate * jax.nn.sigmoid(gate) * up).astype(BF16)

    def expert_out(g, i):
        cols = pl.ds(pl.multiple_of(i * TILE, TILE), TILE)
        h = hid[g, :, :, cols].reshape(NZ * HID, TILE)
        out = jnp.dot(wd[...], h, preferred_element_type=F32).astype(BF16).astype(F32)
        outs[pl.ds(pl.multiple_of(g * GROUP + i * TILE, TILE), TILE), :] = out.T.astype(BF16)

    def send_back(j):
        scatter(outs, ret, o_send, o_recv.at[j], j, 1, pl.ds(0, FEAT))

    def unplace(j):
        rows = offset_rows(j)
        wait_for(ret.at[rows, :], o_recv.at[j])
        got = ret[rows, :].astype(F32).T.astype(BF16)
        return jnp.dot(got, place[rows, :], preferred_element_type=F32)

    def each(n, f):
        def one(i, carry):
            f(i)
            return carry

        lax.fori_loop(0, n, one, 0)

    tiles = GROUP // TILE
    pl.semaphore_wait(barrier, NX * NC - 1 + NZ - 1)

    begin(plain_ring)
    for j in range(NX):
        put_own(j)

    def plain_work(s):
        for j in range(GX):
            put_pair(j, s)

        @pl.when(s == 1)
        def _():
            for load in loads:
                load.wait()

        for k in range(STEPS - 2):
            @pl.when(s == k + 1)
            def _():
                sort_weights(range(NZ * k // (STEPS - 2), NZ * (k + 1) // (STEPS - 2)))

        @pl.when(s == 4)
        def _():
            for g in range(GROUPS):
                wait_for(xr.at[group_rows(g), :], x_recv.at[g])
                turn_in(g)

    run(plain_ring, plain_work, lambda: begin(slotted_ring))
    for j in range(GX):
        put_pair(j, STEPS - 1)
    for p in range(PIECES):
        last(plain_ring, p)
    for j in range(NX):
        put_far(j)

    def slotted_work(s):
        for j in range(GX, NX):
            put_pair(j, s)

        @pl.when(s == 4)
        def _():
            wait_for(pr.at[group_rows(0), :], ps_recv.at[0])

        @pl.when(s >= 4)
        def _():
            placed_in(0, 2 * (s - 4))
            placed_in(0, 2 * (s - 4) + 1)

    run(slotted_ring, slotted_work, lambda: None)
    for p in range(2):
        last(slotted_ring, p)
    each(tiles, lambda i: slotted_in(0, i))
    begin(hid_rings[0])
    for j in range(GX, NX):
        put_pair(j, STEPS - 1)
    for p in range(2, PIECES):
        last(slotted_ring, p)

    def hid_work_0(s):
        @pl.when(s == 3)
        def _():
            wait_for(pr.at[group_rows(1), :], ps_recv.at[1])

        @pl.when(s >= 3)
        def _():
            i = s - 3
            placed_in(1, i)
            slotted_in(1, i)

    def hid_after_0():
        for i in range(STEPS - 4, tiles):
            placed_in(1, i)
            slotted_in(1, i)
        begin(hid_rings[1])

    run(hid_rings[0], hid_work_0, hid_after_0)
    for p in range(PIECES):
        last(hid_rings[0], p)

    def hid_work_1(s):
        @pl.when(s <= 3)
        def _():
            expert_out(0, 2 * s - 2)
            expert_out(0, 2 * s - 1)

        @pl.when(s == 4)
        def _():
            for j in range(GX):
                send_back(j)

        @pl.when(s == 6)
        def _():
            pairs[...] = unplace(0) + unplace(1)

    run(hid_rings[1], hid_work_1, lambda: None)
    for j in range(GX):
        for p in range(2 * j, 2 * j + 2):
            last(hid_rings[1], p)
        each(tiles // GX, lambda i: expert_out(1, j * (tiles // GX) + i))
        send_back(GX + j)
    pairs[...] += unplace(2)
    pairs[...] += unplace(3)
    for i in range(ROWS // TILE):
        cols = pl.ds(i * TILE, TILE)
        parts[mz, pl.ds(i, 1), :] = jnp.sum(pairs[:, cols] * cot_ref[:, cols].astype(F32), axis=0, keepdims=True)

    def share(k, carry):
        pltpu.make_async_remote_copy(
            src_ref=parts.at[mz],
            dst_ref=parts.at[mz],
            send_sem=p_send,
            recv_sem=p_recv,
            device_id=(mx, mc, lax.rem(mz + k, NZ)),
            device_id_type=MESH,
        ).start()
        return carry

    lax.fori_loop(1, NZ, share, 0)
    mix_ref[...] = (pairs[...] * wts_ref[...]).astype(BF16)
    own = pl.ds(CAP, SLOTS - CAP)
    wait_for(xs.at[own, :], x_send)
    wait_for(ps.at[own, :], ps_send)
    wait_for(outs.at[own, :], o_send)
    for ring in [plain_ring, slotted_ring] + hid_rings:
        ring_sent(ring)
    others = parts.at[pl.ds(0, NZ - 1)]
    wait_for(others, p_recv)
    wait_for(others, p_send)
    route_ref[...] = jnp.sum(parts[...], axis=0) * D ** (-0.5)


def per_device(tokens, route_ids, route_weights, cotangent, w_gate, w_up, w_down):
    vmem, hbm = pl.BlockSpec(memory_space=pltpu.VMEM), pl.BlockSpec(memory_space=pl.ANY)
    dma = pltpu.SemaphoreType.DMA
    ring_sems = (2, STEPS, PIECES)
    mixed, route = pl.pallas_call(
        kernel,
        out_shape=(jax.ShapeDtypeStruct((FEAT, ROWS), BF16), jax.ShapeDtypeStruct((8, TILE), F32)),
        in_specs=[vmem] * 4 + [hbm] * 3,
        out_specs=(vmem, vmem),
        scratch_shapes=[
            pltpu.VMEM((HID, D), BF16),
            pltpu.VMEM((HID, D), BF16),
            pltpu.VMEM((FEAT, NZ * HID), BF16),
            pltpu.VMEM((2 * HID, NZ * PLAIN), BF16),
            pltpu.VMEM((2 * HID, NZ * SLOTTED), BF16),
            pltpu.VMEM((SLOTS, ROWS), BF16),
            pltpu.VMEM((SLOTS, FEAT), BF16),
            pltpu.VMEM((SLOTS, FEAT), BF16),
            pltpu.VMEM((SLOTS, FAR + PLAIN), BF16),
            pltpu.VMEM((SLOTS, FAR + PLAIN), BF16),
            pltpu.VMEM((NZ, PLAIN, ROWS), BF16),
            pltpu.VMEM((NZ, SLOTTED, SLOTS), BF16),
            pltpu.VMEM((2 * HID, SLOTS), F32),
            pltpu.VMEM((GROUPS, NZ, HID, GROUP), BF16),
            pltpu.VMEM((SLOTS, FEAT), BF16),
            pltpu.VMEM((SLOTS, FEAT), BF16),
            pltpu.VMEM((FEAT, ROWS), F32),
            pltpu.VMEM((NZ, 8, TILE), F32),
            dma((3,)),
            dma,
            dma((GROUPS,)),
            dma,
            dma((GROUPS,)),
            dma,
            dma(ring_sems),
            dma,
            dma(ring_sems),
            dma((GROUPS,)),
            dma((GROUPS, *ring_sems)),
            dma,
            dma((NX,)),
            dma,
            dma,
        ],
        compiler_params=pltpu.CompilerParams(
            collective_id=0, has_side_effects=True, vmem_limit_bytes=60 * 2**20
        ),
    )(
        route_ids.reshape(1, ROWS),
        route_weights.reshape(1, ROWS),
        tokens.T,
        cotangent.T,
        w_gate[0],
        w_up[0],
        w_down[0],
    )
    return mixed.T, route.reshape(ROWS, 1)


def solution(mesh):
    in_specs = (
        P(("tensor", "context"), "dp"),
        P(("tensor", "context"), None),
        P(("tensor", "context"), None),
        P(("tensor", "context"), "dp"),
        P(("tensor", "context"), "dp", None),
        P(("tensor", "context"), "dp", None),
        P(("tensor", "context"), "dp", None),
    )
    out_specs = (P(("tensor", "context"), "dp"), P(("tensor", "context"), None))
    return jax.shard_map(
        per_device, mesh=mesh, in_specs=in_specs, out_specs=out_specs, check_vma=False
    )
```

time: 249 us -> 218 us (0.88)
  Pallas kernels: 243 us -> 214 us
    pallas_call x1, Pallas kernels: 243 us -> 214 us  [per_device(): pl.pallas_call(kernel, out_shape=(jax.ShapeDtypeStruct((FEAT, ROWS), BF16...]
where the time goes in v2:
time: 218 us
  Pallas kernels  214 us (98%)
  local copies, waits for them, and re-layouts  3.09 us (1%)
    pallas_call x1, Pallas kernels, per_device(): pl.pallas_call(kernel, out_shape=(jax.ShapeDtypeStruct((FEAT, ROWS), BF16...  214 us

profile of v2, /device:TPU:1, one launch (start us, length us, event | category | flops | bytes accessed | tf_op | source)
XLA Modules:
  0.0 217.9 jit_solution(3721903379589519184)
XLA Ops:
  0.6 214.1 %shard_map.86 = (bf16[224,1024]{1,0:T(8,128)(2,1)}, f32[8,128]{1,0:T(8,128)}) custom-call(s32[1,1024]{1,0:T(1,128)} %bitcast.16, f32[1,1024]{1,0:T(1,128)} %bitcast.17, bf16[224,1024]{1,0:T(8,128)(2,1)} %bitcast.12, bf16[224,1024]{1,0:T(8,128)(2,1)} %bitcast.13, bf16[160,3584]{1,0:T(8,128)(2,1)} %bitcast.9, bf16[160,3584]{1,0:T(8,128)(2,1)} %bitcast.10, ...), custom_call_target="tpu_custom_call" | custom-call | tf_op jit(solution)/shard_map/pallas_call | solution.py:374
  214.8 1.8 copy.11
  216.6 1.3 copy.12

commit v3 on v2

v3 whole, which is shorter than its diff:
```python
import jax
import jax.numpy as jnp
from jax import lax
from jax.experimental import pallas as pl
from jax.experimental.pallas import tpu as pltpu
from jax.sharding import PartitionSpec as P

MESH = pl.DeviceIdType.MESH
F32, BF16 = jnp.float32, jnp.bfloat16
NX, NC, NZ = 4, 8, 16
OFFSETS = (0, 2, 1, 3)
ROWS, FEAT, HID, D = 1024, 224, 160, 3584
CAP = 48
XSLOTS = NC * CAP
GX = 2
GROUP = GX * XSLOTS
GROUPS = NX // GX
SLOTS = NX * XSLOTS
TILE = 128
NT = (((1,), (1,)), ((), ()))
PLAIN = 128
SLOTTED = FEAT - PLAIN
PAIR = 2 * PLAIN
STEPS = NZ // 2
FAR = (STEPS - 1) * PAIR
PLAIN_PIECES = tuple((32 * p, 32, 0, ROWS) for p in range(4))
SLOTTED_PIECES = tuple((48 * (p % 2), 48, GROUP * (p // 2), GROUP) for p in range(4))
HID_PIECES = tuple((80 * (p % 2), 80, XSLOTS * (p // 2), XSLOTS) for p in range(4))
PIECES = 4


def kernel(
    ids_ref, wts_ref, tok_in, cot_ref, wg_hbm, wu_hbm, wd_hbm,
    mix_ref, route_ref,
    wg, wu, wd, w_placed, w_slot, place, xs, xr, ps, pr, plain, slotted, acc, hid, outs, ret, pairs, parts,
    w_sem, x_send, x_recv, ps_send, ps_recv, a_send, a_recv, b_send, b_recv, h_send, h_recv,
    o_send, o_recv, p_send, p_recv,
):
    mx, mc, mz = lax.axis_index("tensor"), lax.axis_index("context"), lax.axis_index("dp")
    above, below = lax.rem(mz + 1, NZ), lax.rem(mz + NZ - 1, NZ)

    barrier = pltpu.get_barrier_semaphore()

    def greet(k, carry):
        p = lax.rem(mx * NC + mc + k, NX * NC)
        pl.semaphore_signal(barrier, inc=1, device_id=(p // NC, lax.rem(p, NC), mz), device_id_type=MESH)
        return carry

    for plane in (above, below):
        pl.semaphore_signal(barrier, inc=1, device_id=(mx, mc, plane), device_id_type=MESH)
    lax.fori_loop(1, NX * NC, greet, 0)
    loads = [
        pltpu.make_async_copy(src, dst, w_sem.at[i])
        for i, (src, dst) in enumerate(((wg_hbm, wg), (wu_hbm, wu), (wd_hbm, wd)))
    ]
    for load in loads:
        load.start()

    def piece_at(j, c):
        return pl.ds(pl.multiple_of((j * NC + c) * CAP, 16), CAP)

    def scatter(src, dst, send, recv, j, toward, lanes):
        tx = lax.rem(mx + NX + toward * OFFSETS[j], NX)

        def one(k, carry):
            c = lax.rem(mc + k, NC)
            pltpu.make_async_remote_copy(
                src_ref=src.at[piece_at(j, c), lanes],
                dst_ref=dst.at[piece_at(j, mc), lanes],
                send_sem=send,
                recv_sem=recv,
                device_id=(tx, c, mz),
                device_id_type=MESH,
            ).start()
            return carry

        if j == 0:
            pltpu.make_async_copy(src.at[piece_at(0, mc), lanes], dst.at[piece_at(0, mc), lanes], recv).start()
        lax.fori_loop(1 if j == 0 else 0, NC, one, 0)

    def wait_for(part, sem):
        pltpu.make_async_copy(part, part, sem).wait()

    def offset_rows(j):
        return pl.ds(j * XSLOTS, XSLOTS)

    def group_rows(g):
        return pl.ds(g * GROUP, GROUP)

    def part_of(ring, way, s, p):
        origin = lax.rem(mz + NZ - s, NZ) if way == 0 else lax.rem(mz + s, NZ)
        r, rows, c, cols = ring["pieces"][p]
        return ring["buf"].at[(*ring["at"], origin, pl.ds(r, rows), pl.ds(c, cols))]

    def forward(ring, way, s, p):
        part = part_of(ring, way, s, p)
        src = part
        if isinstance(s, int) and s == 0 and "own" in ring:
            r, rows, c, cols = ring["pieces"][p]
            src = ring["own"].at[pl.ds(r, rows), pl.ds(c, cols)]
        pltpu.make_async_remote_copy(
            src_ref=src,
            dst_ref=part,
            send_sem=ring["send"],
            recv_sem=ring["recv"].at[(*ring["at"], way, s, p)],
            device_id=(mx, mc, above if way == 0 else below),
            device_id_type=MESH,
        ).start()

    def arrived(ring, way, s, p):
        wait_for(part_of(ring, way, s, p), ring["recv"].at[(*ring["at"], way, s - 1, p)])

    def begin(ring):
        for p in range(PIECES):
            for way in range(2):
                forward(ring, way, 0, p)

    def run(ring, work, after):
        def step(s, carry):
            for p in range(PIECES):
                for way in range(2):
                    arrived(ring, way, s, p)
                    forward(ring, way, s, p)
            work(s)
            return carry

        lax.fori_loop(1, STEPS - 1, step, 0)
        for p in range(PIECES):
            for way in range(2):
                arrived(ring, way, STEPS - 1, p)
                if p % 2 == way:
                    forward(ring, way, STEPS - 1, p)
        after()

    def last(ring, p):
        arrived(ring, p % 2, STEPS, p)

    def ring_sent(ring):
        wait_for(ring["buf"].at[(*ring["at"], pl.ds(0, NZ - 1))], ring["send"])

    plain_ring = dict(buf=plain, at=(), send=a_send, recv=a_recv, pieces=PLAIN_PIECES, own=tok_in)
    slotted_ring = dict(buf=slotted, at=(), send=b_send, recv=b_recv, pieces=SLOTTED_PIECES)
    hid_rings = [
        dict(buf=hid, at=(g,), send=h_send.at[g], recv=h_recv, pieces=HID_PIECES) for g in range(GROUPS)
    ]

    def put_own(j):
        rows = offset_rows(j)
        at = lax.broadcasted_iota(jnp.int32, (XSLOTS, ROWS), 0) + j * XSLOTS
        place[rows, :] = (at == slot).astype(F32).astype(BF16)
        xs[rows, :] = lax.dot_general(place[rows, :], tok_in[...], NT, preferred_element_type=F32).astype(BF16)
        scatter(xs, xr, x_send, x_recv.at[j // GX], j, -1, pl.ds(0, FEAT))

    def put_pair(j, s):
        lanes = pl.ds(pl.multiple_of((s - 1) * PAIR, PAIR), PAIR)
        rows = offset_rows(j)
        pair = jnp.concatenate([plain[lax.rem(mz + NZ - s, NZ)], plain[lax.rem(mz + s, NZ)]], axis=0)
        ps[rows, lanes] = lax.dot_general(place[rows, :], pair, NT, preferred_element_type=F32).astype(BF16)
        scatter(ps, pr, ps_send, ps_recv.at[j // GX], j, -1, lanes)

    def put_far(j):
        lanes = pl.ds(FAR, PLAIN)
        rows = offset_rows(j)
        far = plain[lax.rem(mz + STEPS, NZ)]
        ps[rows, lanes] = lax.dot_general(place[rows, :], far, NT, preferred_element_type=F32).astype(BF16)
        scatter(ps, pr, ps_send, ps_recv.at[j // GX], j, -1, lanes)

    def sort_weights(planes):
        for o in planes:
            away = lax.rem(o + NZ - mz, NZ)
            half = away // STEPS
            lane = lax.rem((1 - half) * (PAIR * away - PLAIN) + half * PAIR * (NZ - 1 - away) + NZ * PLAIN, NZ * PLAIN)
            at = pl.ds(pl.multiple_of(lane, TILE), PLAIN)
            for rows, w in ((pl.ds(0, HID), wg), (pl.ds(HID, HID), wu)):
                w_placed[rows, at] = w[:, o * FEAT : o * FEAT + PLAIN]
                w_slot[rows, o * SLOTTED : (o + 1) * SLOTTED] = w[:, o * FEAT + PLAIN : (o + 1) * FEAT]

    def turn_in(g):
        slotted[mz, :, g * GROUP : (g + 1) * GROUP] = xr[group_rows(g), pl.ds(PLAIN, SLOTTED)].astype(F32).T.astype(BF16)

    def placed_in(g, i):
        start = pl.multiple_of(g * GROUP + i * TILE, TILE)
        rows, cols = pl.ds(start, TILE), pl.ds(start, TILE)
        acc[:, cols] = lax.dot_general(
            w_placed[:, pl.ds(0, FAR + PLAIN)], pr[rows, :], NT, preferred_element_type=F32
        ) + lax.dot_general(
            w_placed[:, pl.ds(FAR + PLAIN, PLAIN)], xr[rows, pl.ds(0, PLAIN)], NT, preferred_element_type=F32
        )

    def slotted_in(g, i, width=TILE):
        start = pl.multiple_of(g * GROUP + i * width, TILE)
        cols = pl.ds(start, width)
        x = slotted[:, :, cols].reshape(NZ * SLOTTED, width)
        both = acc[:, cols] + jnp.dot(w_slot[...], x, preferred_element_type=F32)
        gate, up = both[:HID], both[HID:]
        hid[g, mz, :, pl.ds(pl.multiple_of(i * width, TILE), width)] = (gate * jax.nn.sigmoid(gate) * up).astype(BF16)

    def expert_out(g, i, width=TILE):
        cols = pl.ds(pl.multiple_of(i * width, TILE), width)
        h = hid[g, :, :, cols].reshape(NZ * HID, width)
        out = jnp.dot(wd[...], h, preferred_element_type=F32).astype(BF16).astype(F32)
        outs[pl.ds(pl.multiple_of(g * GROUP + i * width, TILE), width), :] = out.T.astype(BF16)

    def send_back(j):
        scatter(outs, ret, o_send, o_recv.at[j], j, 1, pl.ds(0, FEAT))

    def unplace(j):
        rows = offset_rows(j)
        wait_for(ret.at[rows, :], o_recv.at[j])
        got = ret[rows, :].astype(F32).T.astype(BF16)
        return jnp.dot(got, place[rows, :], preferred_element_type=F32)

    tiles = GROUP // TILE
    pl.semaphore_wait(barrier, NX * NC - 1 + 2)

    begin(plain_ring)
    ids = ids_ref[...]
    offset = lax.rem(mx + NX - ids // NC, NX)
    rel = (lax.rem(offset, 2) * 2 + offset // 2) * NC + lax.rem(ids, NC)
    expert = lax.broadcasted_iota(jnp.int32, (NX * NC, TILE), 0)
    lower = (
        lax.broadcasted_iota(jnp.int32, (TILE, TILE), 0) < lax.broadcasted_iota(jnp.int32, (TILE, TILE), 1)
    ).astype(F32).astype(BF16)
    seen = jnp.zeros((NX * NC, 1), F32)
    slots = []
    for i in range(ROWS // TILE):
        r = rel[:, i * TILE : (i + 1) * TILE]
        onehot = (expert == r).astype(F32)
        before = jnp.dot(onehot.astype(BF16), lower, preferred_element_type=F32) + seen
        position = jnp.sum(onehot * before, axis=0, keepdims=True)
        slots.append(r * CAP + position.astype(jnp.int32))
        seen = seen + jnp.sum(onehot, axis=1, keepdims=True)
    slot = jnp.concatenate(slots, axis=1)
    for j in range(NX):
        put_own(j)

    def plain_work(s):
        for j in range(GX):
            put_pair(j, s)

        @pl.when(s == 1)
        def _():
            for load in loads:
                load.wait()

        for k in range(STEPS - 2):
            @pl.when(s == k + 1)
            def _():
                sort_weights(range(NZ * k // (STEPS - 2), NZ * (k + 1) // (STEPS - 2)))

        @pl.when(s == 4)
        def _():
            for g in range(GROUPS):
                wait_for(xr.at[group_rows(g), :], x_recv.at[g])
                turn_in(g)

    run(plain_ring, plain_work, lambda: begin(slotted_ring))
    for j in range(GX):
        put_pair(j, STEPS - 1)
    for p in range(PIECES):
        last(plain_ring, p)
    for j in range(NX):
        put_far(j)

    def slotted_work(s):
        for j in range(GX, NX):
            put_pair(j, s)

        @pl.when(s == 4)
        def _():
            wait_for(pr.at[group_rows(0), :], ps_recv.at[0])

        @pl.when(s >= 4)
        def _():
            placed_in(0, 2 * (s - 4))
            placed_in(0, 2 * (s - 4) + 1)

    run(slotted_ring, slotted_work, lambda: None)
    for p in range(2):
        last(slotted_ring, p)
    for half in range(GX):
        slotted_in(0, half, XSLOTS)
        for p in range(2 * half, 2 * half + 2):
            for way in range(2):
                forward(hid_rings[0], way, 0, p)
    for j in range(GX, NX):
        put_pair(j, STEPS - 1)
    for p in range(2, PIECES):
        last(slotted_ring, p)

    def hid_work_0(s):
        @pl.when(s == 3)
        def _():
            wait_for(pr.at[group_rows(1), :], ps_recv.at[1])

        @pl.when(s >= 3)
        def _():
            i = s - 3
            placed_in(1, i)
            slotted_in(1, i)

    def hid_after_0():
        for i in range(STEPS - 4, tiles):
            placed_in(1, i)
            slotted_in(1, i)
        begin(hid_rings[1])

    run(hid_rings[0], hid_work_0, hid_after_0)
    for p in range(PIECES):
        last(hid_rings[0], p)

    def hid_work_1(s):
        @pl.when(s <= 3)
        def _():
            expert_out(0, 2 * s - 2)
            expert_out(0, 2 * s - 1)

        @pl.when(s == 4)
        def _():
            for j in range(GX):
                send_back(j)

        @pl.when(s == 6)
        def _():
            pairs[...] = unplace(0) + unplace(1)

    run(hid_rings[1], hid_work_1, lambda: None)
    for j in range(GX):
        for p in range(2 * j, 2 * j + 2):
            last(hid_rings[1], p)
        expert_out(1, j, XSLOTS)
        send_back(GX + j)
    pairs[...] += unplace(2)
    pairs[...] += unplace(3)
    for i in range(ROWS // TILE):
        cols = pl.ds(i * TILE, TILE)
        parts[mz, pl.ds(i, 1), :] = jnp.sum(pairs[:, cols] * cot_ref[:, cols].astype(F32), axis=0, keepdims=True)

    def share(k, carry):
        pltpu.make_async_remote_copy(
            src_ref=parts.at[mz],
            dst_ref=parts.at[mz],
            send_sem=p_send,
            recv_sem=p_recv,
            device_id=(mx, mc, lax.rem(mz + k, NZ)),
            device_id_type=MESH,
        ).start()
        return carry

    lax.fori_loop(1, NZ, share, 0)
    mix_ref[...] = (pairs[...] * wts_ref[...]).astype(BF16)
    own = pl.ds(CAP, SLOTS - CAP)
    wait_for(xs.at[own, :], x_send)
    wait_for(ps.at[own, :], ps_send)
    wait_for(outs.at[own, :], o_send)
    for ring in [plain_ring, slotted_ring] + hid_rings:
        ring_sent(ring)
    others = parts.at[pl.ds(0, NZ - 1)]
    wait_for(others, p_recv)
    wait_for(others, p_send)
    route_ref[...] = jnp.sum(parts[...], axis=0) * D ** (-0.5)


def hand_over(mix_in, route_in, mix_out, route_out):
    mix_out[...] = mix_in[...]
    route_out[...] = route_in[...]


def per_device(tokens, route_ids, route_weights, cotangent, w_gate, w_up, w_down):
    vmem, hbm = pl.BlockSpec(memory_space=pltpu.VMEM), pl.BlockSpec(memory_space=pl.ANY)
    dma = pltpu.SemaphoreType.DMA
    ring_sems = (2, STEPS, PIECES)
    out_shape = (jax.ShapeDtypeStruct((FEAT, ROWS), BF16), jax.ShapeDtypeStruct((8, TILE), F32))
    results = pl.pallas_call(
        kernel,
        out_shape=out_shape,
        in_specs=[vmem] * 4 + [hbm] * 3,
        out_specs=(vmem, vmem),
        scratch_shapes=[
            pltpu.VMEM((HID, D), BF16),
            pltpu.VMEM((HID, D), BF16),
            pltpu.VMEM((FEAT, NZ * HID), BF16),
            pltpu.VMEM((2 * HID, NZ * PLAIN), BF16),
            pltpu.VMEM((2 * HID, NZ * SLOTTED), BF16),
            pltpu.VMEM((SLOTS, ROWS), BF16),
            pltpu.VMEM((SLOTS, FEAT), BF16),
            pltpu.VMEM((SLOTS, FEAT), BF16),
            pltpu.VMEM((SLOTS, FAR + PLAIN), BF16),
            pltpu.VMEM((SLOTS, FAR + PLAIN), BF16),
            pltpu.VMEM((NZ, PLAIN, ROWS), BF16),
            pltpu.VMEM((NZ, SLOTTED, SLOTS), BF16),
            pltpu.VMEM((2 * HID, SLOTS), F32),
            pltpu.VMEM((GROUPS, NZ, HID, GROUP), BF16),
            pltpu.VMEM((SLOTS, FEAT), BF16),
            pltpu.VMEM((SLOTS, FEAT), BF16),
            pltpu.VMEM((FEAT, ROWS), F32),
            pltpu.VMEM((NZ, 8, TILE), F32),
            dma((3,)),
            dma,
            dma((GROUPS,)),
            dma,
            dma((GROUPS,)),
            dma,
            dma(ring_sems),
            dma,
            dma(ring_sems),
            dma((GROUPS,)),
            dma((GROUPS, *ring_sems)),
            dma,
            dma((NX,)),
            dma,
            dma,
        ],
        compiler_params=pltpu.CompilerParams(
            collective_id=0, has_side_effects=True, vmem_limit_bytes=60 * 2**20
        ),
    )(
        route_ids.reshape(1, ROWS),
        route_weights.reshape(1, ROWS),
        tokens.T,
        cotangent.T,
        w_gate[0],
        w_up[0],
        w_down[0],
    )
    mixed, route = pl.pallas_call(
        hand_over,
        out_shape=out_shape,
        in_specs=[vmem] * 2,
        out_specs=(vmem, vmem),
    )(*results)
    return mixed.T, route.reshape(ROWS, 1)


def solution(mesh):
    in_specs = (
        P(("tensor", "context"), "dp"),
        P(("tensor", "context"), None),
        P(("tensor", "context"), None),
        P(("tensor", "context"), "dp"),
        P(("tensor", "context"), "dp", None),
        P(("tensor", "context"), "dp", None),
        P(("tensor", "context"), "dp", None),
    )
    out_specs = (P(("tensor", "context"), "dp"), P(("tensor", "context"), None))
    return jax.shard_map(
        per_device, mesh=mesh, in_specs=in_specs, out_specs=out_specs, check_vma=False
    )
```

time: 218 us -> 210 us (0.963)
  Pallas kernels: 214 us -> 209 us
  local copies, waits for them, and re-layouts: 3.09 us -> 0 us
    pallas_call x1 -> x2, Pallas kernels: 214 us -> 209 us  [the longest x1 207 us: per_device(): pl.pallas_call(kernel, out_shape=out_shape, in_specs=[vmem] * 4 + [hbm] *...]
    unnamed x2 -> x0, local copies, waits for them, and re-layouts: 3.09 us -> none
where the time goes in v3:
time: 210 us; the launch traced here: 209 us
  Pallas kernels  209 us (100%)
    pallas_call x1, Pallas kernels, per_device(): pl.pallas_call(kernel, out_shape=out_shape, in_specs=[vmem] * 4 + [hbm] *...  207 us

profile of v3, /device:TPU:1, one launch (start us, length us, event | category | flops | bytes accessed | tf_op | source)
XLA Modules:
  0.0 209.5 jit_solution(5956249068838110634)
XLA Ops:
  0.6 207.0 %shard_map.86 = (bf16[224,1024]{1,0:T(8,128)(2,1)}, f32[8,128]{1,0:T(8,128)}) custom-call(s32[1,1024]{1,0:T(1,128)} %bitcast.14, f32[1,1024]{1,0:T(1,128)} %bitcast.15, bf16[224,1024]{1,0:T(8,128)(2,1)} %bitcast.12, bf16[224,1024]{1,0:T(8,128)(2,1)} %bitcast.13, bf16[160,3584]{1,0:T(8,128)(2,1)} %bitcast.9, bf16[160,3584]{1,0:T(8,128)(2,1)} %bitcast.10, ...), custom_call_target="tpu_custom_call" | custom-call | tf_op jit(solution)/shard_map/pallas_call | solution.py:374
  207.6 1.8 shard_map.87

commit v4 on v3

--- a/solution.py
+++ b/solution.py
@@ -8,7 +8,7 @@
 MESH = pl.DeviceIdType.MESH
 F32, BF16 = jnp.float32, jnp.bfloat16
 NX, NC, NZ = 4, 8, 16
-OFFSETS = (0, 2, 1, 3)
+OFFSETS = (1, 3, 2, 0)
 ROWS, FEAT, HID, D = 1024, 224, 160, 3584
 CAP = 48
 XSLOTS = NC * CAP
@@ -30,9 +30,9 @@
 
 
 def kernel(
-    ids_ref, wts_ref, tok_in, cot_ref, wg_hbm, wu_hbm, wd_hbm,
+    ids_ref, wts_ref, tok_hbm, cot_hbm, wg_hbm, wu_hbm, wd_hbm,
     mix_ref, route_ref,
-    wg, wu, wd, w_placed, w_slot, place, xs, xr, ps, pr, plain, slotted, acc, hid, outs, ret, pairs, parts,
+    tok_in, cot_ref, wg, wu, wd, w_placed, w_slot, place, xs, xr, ps, pr, plain, slotted, acc, hid, outs, ret, pairs, parts,
     w_sem, x_send, x_recv, ps_send, ps_recv, a_send, a_recv, b_send, b_recv, h_send, h_recv,
     o_send, o_recv, p_send, p_recv,
 ):
@@ -51,7 +51,7 @@
     lax.fori_loop(1, NX * NC, greet, 0)
     loads = [
         pltpu.make_async_copy(src, dst, w_sem.at[i])
-        for i, (src, dst) in enumerate(((wg_hbm, wg), (wu_hbm, wu), (wd_hbm, wd)))
+        for i, (src, dst) in enumerate(((tok_hbm, tok_in), (wg_hbm, wg), (wu_hbm, wu), (wd_hbm, wd), (cot_hbm, cot_ref)))
     ]
     for load in loads:
         load.start()
@@ -74,9 +74,10 @@
             ).start()
             return carry
 
-        if j == 0:
-            pltpu.make_async_copy(src.at[piece_at(0, mc), lanes], dst.at[piece_at(0, mc), lanes], recv).start()
-        lax.fori_loop(1 if j == 0 else 0, NC, one, 0)
+        here = OFFSETS[j] == 0
+        if here:
+            pltpu.make_async_copy(src.at[piece_at(j, mc), lanes], dst.at[piece_at(j, mc), lanes], recv).start()
+        lax.fori_loop(int(here), NC, one, 0)
 
     def wait_for(part, sem):
         pltpu.make_async_copy(part, part, sem).wait()
@@ -213,10 +214,12 @@
     tiles = GROUP // TILE
     pl.semaphore_wait(barrier, NX * NC - 1 + 2)
 
+    loads[0].wait()
     begin(plain_ring)
     ids = ids_ref[...]
     offset = lax.rem(mx + NX - ids // NC, NX)
-    rel = (lax.rem(offset, 2) * 2 + offset // 2) * NC + lax.rem(ids, NC)
+    odd = lax.rem(offset, 2)
+    rel = (odd * (offset // 2) + (1 - odd) * (NX - 1 - offset // 2)) * NC + lax.rem(ids, NC)
     expert = lax.broadcasted_iota(jnp.int32, (NX * NC, TILE), 0)
     lower = (
         lax.broadcasted_iota(jnp.int32, (TILE, TILE), 0) < lax.broadcasted_iota(jnp.int32, (TILE, TILE), 1)
@@ -231,16 +234,20 @@
         slots.append(r * CAP + position.astype(jnp.int32))
         seen = seen + jnp.sum(onehot, axis=1, keepdims=True)
     slot = jnp.concatenate(slots, axis=1)
-    for j in range(NX):
+    for j in range(GX):
         put_own(j)
 
     def plain_work(s):
         for j in range(GX):
             put_pair(j, s)
+        for j in range(GX, NX):
+            @pl.when(s == j - 1)
+            def _():
+                put_own(j)
 
         @pl.when(s == 1)
         def _():
-            for load in loads:
+            for load in loads[1:]:
                 load.wait()
 
         for k in range(STEPS - 2):
@@ -248,7 +255,7 @@
             def _():
                 sort_weights(range(NZ * k // (STEPS - 2), NZ * (k + 1) // (STEPS - 2)))
 
-        @pl.when(s == 4)
+        @pl.when(s == 6)
         def _():
             for g in range(GROUPS):
                 wait_for(xr.at[group_rows(g), :], x_recv.at[g])
@@ -374,9 +381,11 @@
     results = pl.pallas_call(
         kernel,
         out_shape=out_shape,
-        in_specs=[vmem] * 4 + [hbm] * 3,
+        in_specs=[vmem] * 2 + [hbm] * 5,
         out_specs=(vmem, vmem),
         scratch_shapes=[
+            pltpu.VMEM((FEAT, ROWS), BF16),
+            pltpu.VMEM((FEAT, ROWS), BF16),
             pltpu.VMEM((HID, D), BF16),
             pltpu.VMEM((HID, D), BF16),
             pltpu.VMEM((FEAT, NZ * HID), BF16),
@@ -395,7 +404,7 @@
             pltpu.VMEM((SLOTS, FEAT), BF16),
             pltpu.VMEM((FEAT, ROWS), F32),
             pltpu.VMEM((NZ, 8, TILE), F32),
-            dma((3,)),
+            dma((5,)),
             dma,
             dma((GROUPS,)),
             dma,

time: 210 us -> 209 us (level)
  no operation moved by 1% of the time
where the time goes in v4:
time: 209 us; the launch traced here: 208 us
  Pallas kernels  208 us (100%)
    pallas_call x1, Pallas kernels, per_device(): pl.pallas_call(kernel, out_shape=out_shape, in_specs=[vmem] * 2 + [hbm] *...  206 us

profile of v4, /device:TPU:1, one launch (start us, length us, event | category | flops | bytes accessed | tf_op | source)
XLA Modules:
  0.0 208.4 jit_solution(5379074138028268713)
XLA Ops:
  0.6 206.0 %shard_map.86 = (bf16[224,1024]{1,0:T(8,128)(2,1)}, f32[8,128]{1,0:T(8,128)}) custom-call(s32[1,1024]{1,0:T(1,128)} %bitcast.14, f32[1,1024]{1,0:T(1,128)} %bitcast.15, bf16[224,1024]{1,0:T(8,128)(2,1)} %bitcast.12, bf16[224,1024]{1,0:T(8,128)(2,1)} %bitcast.13, bf16[160,3584]{1,0:T(8,128)(2,1)} %bitcast.9, bf16[160,3584]{1,0:T(8,128)(2,1)} %bitcast.10, ...), custom_call_target="tpu_custom_call" | custom-call | tf_op jit(solution)/shard_map/pallas_call | solution.py:381
  206.6 1.8 shard_map.87
